TPU v7x, 512 devices: a whole 4x8x8 slice. The times are simulated.
512 devices in a mesh: dp: 32 (over y, x), tensor: 16 (over z, core).
Axes of the slice: x: 4, y: 8, z: 8, core: 2. Of those that a mesh axis runs over, the one named last changes fastest.
Arguments:
- hidden_in: bfloat16 [2048, 12288], P('dp'), may hold values from -6 to 6
- norm_gain: bfloat16 [12288], replicated, may hold values from 0.099609375 to 1.8984375
- norm_shift: bfloat16 [12288], replicated, may hold values from -3 to 3
- up_weight: bfloat16 [12288, 24576], P('dp', 'tensor'), may hold values from -0.0546875 to 0.0546875
- up_bias: bfloat16 [24576], P('tensor'), may hold values from -3 to 3
- down_weight: bfloat16 [24576, 12288], P('tensor', 'dp'), may hold values from -0.09375 to 0.09375
- down_bias: bfloat16 [12288], P('tensor'), may hold values from -3 to 3
- active: int32 [64, 16, 4], P(None, 'tensor'), may hold values from 0 to 11, as said below
- counts: int32 [64, 16], P(None, 'tensor'), may hold values from 1 to 4, as said below
Outputs:
- hidden_out: bfloat16 [2048, 12288], P('dp', 'tensor')
Inputs may be any that keep to these rules, and one draw needn't show every extreme that they name: The 4 entries of each list are distinct; only the first counts entries are active. `counts`: every row group has a list with all 4 slots valid.
All inputs are finite; a program needn't handle non-finite values.
Results may differ from a plain program's by a relative error of at most 0.022.
Values may be sent and summed in bfloat16 or wider, within the bound.
No kernel may reach another device: no remote copies, remote signals or barrier semaphores. Data moves between devices by JAX's collectives and lax.ppermute only.
A program may use at most 64 MiB of HBM per device.

v0:
```python
import math
import jax
import jax.numpy as jnp
from jax import lax
from jax.sharding import PartitionSpec as P

BLOCK = 128
GROUP = 32


def in_blocks(step_fn, arrays):
    total = arrays[0].shape[0]
    per = math.gcd(total, 8)
    stacked = tuple((item.reshape((total // per, per) + item.shape[1:]) for item in arrays))
    result = lax.map(step_fn, stacked)
    return result.reshape((total,) + result.shape[2:])


def select_up(rows, ids, up_table):
    ngroups, slots = ids.shape
    grouped = rows.reshape(ngroups, -1, rows.shape[1])

    def step(pair):
        block_rows, block_ids = pair
        chosen = jnp.take(up_table, block_ids, axis=1)
        return jnp.einsum("grd,dgcb->grcb", block_rows, chosen, preferred_element_type=jnp.float32)

    result = in_blocks(step, (grouped, ids))
    return result.reshape(rows.shape[0], slots * up_table.shape[2])


def select_down(act, ids, down_table):
    ngroups, slots = ids.shape
    grouped = act.reshape(ngroups, -1, slots, down_table.shape[1])

    def step(pair):
        block_act, block_ids = pair
        chosen = jnp.take(down_table, block_ids, axis=0)
        return jnp.einsum("grcb,gcbd->grd", block_act, chosen, preferred_element_type=jnp.float32)

    result = in_blocks(step, (grouped, ids))
    return result.reshape(act.shape[0], down_table.shape[2])


def activate(pre, ids, valid, bias_table):
    ngroups, slots = ids.shape
    own = bias_table.shape[0]
    onehot = (ids[:, :, None] == jnp.arange(own, dtype=jnp.int32)[None, None, :]).astype(
        jnp.float32
    )
    bias_sel = jnp.einsum("gco,ob->gcb", onehot, bias_table, precision=lax.Precision.HIGHEST)
    mask = (jnp.arange(slots, dtype=jnp.int32)[None, :] < valid[:, None]).astype(jnp.float32)
    shaped = pre.reshape(ngroups, -1, slots, bias_table.shape[1])
    result = jnp.maximum(shaped + bias_sel[:, None], 0.0) * mask[:, None, :, None]
    return result.astype(jnp.bfloat16).reshape(pre.shape)


def body(
    hidden_in, norm_gain, norm_shift, up_weight, up_bias, down_weight, down_bias, active, counts
):
    row_dev = hidden_in.shape[0]
    values = hidden_in.astype(jnp.float32)
    center = values - jnp.mean(values, axis=-1, keepdims=True)
    spread = jnp.mean(center * center, axis=-1, keepdims=True)
    normed = (
        center * lax.rsqrt(spread + 1e-05) * norm_gain.astype(jnp.float32)
        + norm_shift.astype(jnp.float32)
    ).astype(jnp.bfloat16)
    columns = lax.all_to_all(normed, "dp", split_axis=1, concat_axis=0, tiled=True)
    d_part = up_weight.shape[0]
    own = up_weight.shape[1] // BLOCK
    up_table = up_weight.reshape(d_part, own, BLOCK)
    down_table = down_weight.reshape(own, BLOCK, d_part)
    bias_table = up_bias.astype(jnp.float32).reshape(own, BLOCK)
    ids = active[:, 0, :]
    valid = counts[:, 0]
    pre_own = lax.psum_scatter(
        select_up(columns, ids, up_table).astype(jnp.bfloat16),
        "dp",
        scatter_dimension=0,
        tiled=True,
    ).astype(jnp.float32)
    per_dev = row_dev // GROUP
    first = lax.axis_index("dp") * per_dev
    own_ids = lax.dynamic_slice_in_dim(ids, first, per_dev, 0)
    own_valid = lax.dynamic_slice_in_dim(valid, first, per_dev, 0)
    act_own = activate(pre_own, own_ids, own_valid, bias_table)
    act = lax.all_gather(act_own, "dp", axis=0, tiled=True)
    branch = select_down(act, ids, down_table)
    branch = branch.astype(jnp.bfloat16)
    returned = lax.all_to_all(branch, "dp", split_axis=0, concat_axis=1, tiled=True)
    summed = lax.psum_scatter(
        returned.astype(jnp.float32).astype(jnp.bfloat16), "tensor", scatter_dimension=1, tiled=True
    ).astype(jnp.float32)
    width = summed.shape[1]
    resid = lax.dynamic_slice_in_dim(hidden_in, lax.axis_index("tensor") * width, width, 1).astype(
        jnp.float32
    )
    return (resid + summed + down_bias.astype(jnp.float32)).astype(jnp.bfloat16)


def solution(mesh):
    placed = (
        P("dp", None),
        P(),
        P(),
        P("dp", "tensor"),
        P("tensor"),
        P("tensor", "dp"),
        P("tensor"),
        P(None, "tensor", None),
        P(None, "tensor"),
    )
    return jax.shard_map(
        body, mesh=mesh, in_specs=placed, out_specs=P("dp", "tensor"), check_vma=False
    )
```

profile of v0, /device:TPU:6, one launch (start us, length us, event | category | flops | bytes accessed | tf_op | source)
XLA Modules:
  0.0 595.1 jit_solution(5143126974400507887)
XLA Ops:
  11.2 10.4 %all-to-all-start = ((bf16[64,32,384]{2,0,1:T(8,128)(2,1)}), bf16[64,32,384]{2,0,1:T(8,128)(2,1)}, u32[]{:S(2)}, u32[]{:S(2)}) async-start(bf16[64,32,384]{2,0,1:T(8,128)(2,1)} %bitcast.85), calls=%async_computation | async-start | bytes 3145728 | tf_op jit(solution)/shard_map/all_to_all | solution.py:69
  24.9 36.1 %all-to-all-done = bf16[64,32,384]{2,0,1:T(8,128)(2,1)} async-done(((bf16[64,32,384]{2,0,1:T(8,128)(2,1)}), bf16[64,32,384]{2,0,1:T(8,128)(2,1)}, u32[]{:S(2)}, u32[]{:S(2)}) %all-to-all-start) | async-done | bytes 1572896 | tf_op jit(solution)/shard_map/all_to_all | solution.py:69
  60.9 51.3 %while.20 = (s32[]{:T(128)}, bf16[8,8,32,4,128]{4,2,3,1,0:T(8,128)(2,1)}, bf16[8,8,32,384]{3,2,1,0:T(8,128)(2,1)}, s32[8,8,4]{1,2,0:T(4,128)S(1)}, bf16[384,12,128]{2,0,1:T(8,128)(2,1)S(1)}, /*index=5*/s32[]{:T(128)}) while((s32[]{:T(128)}, bf16[8,8,32,4,128]{4,2,3,1,0:T(8,128)(2,1)}, bf16[8,8,32,384]{3,2,1,0:T(8,128)(2,1)}, ...), condition=%wide.region_3.4_spmd, body=%wide.region_2.3_spmd.sunk | while | flops 102237472 | bytes 10164557 | solution.py:15
  63.8 3.5 fusion.45
  70.2 3.5 fusion.45
  76.6 3.6 fusion.45
  83.0 3.5 fusion.45
  89.4 3.5 fusion.45
  95.8 3.6 fusion.45
  102.3 3.5 fusion.45
  108.7 3.5 fusion.45
  117.6 219.8 %reduce-scatter.3.cloned.1.call-done = bf16[64,512]{1,0:T(8,128)(2,1)} async-done(((bf16[2048,512]{1,0:T(8,128)(2,1)}), bf16[64,512]{1,0:T(8,128)(2,1)}) %reduce-scatter.3.cloned.1.call-update) | async-done | bytes 65552 | tf_op jit(solution)/shard_map/reduce_scatter | solution.py:77
  339.1 83.5 %all-gather.2.cloned.1.call-done = bf16[2048,512]{1,0:T(8,128)(2,1)} async-done(((bf16[64,512]{1,0:T(8,128)(2,1)}), bf16[2048,512]{1,0:T(8,128)(2,1)}) %all-gather.2.cloned.1.call-update) | async-done | bytes 2097168 | tf_op jit(solution)/shard_map/all_gather | solution.py:88
  422.6 4.0 reshape_reshape.9
  426.6 57.6 %while.21 = (s32[]{:T(128)}, bf16[8,8,32,384]{3,2,1,0:T(8,128)(2,1)}, bf16[8,8,32,4,128]{4,3,2,1,0:T(4,128)(2,1)}, s32[8,8,4]{1,2,0:T(4,128)S(1)}, bf16[12,128,384]{2,1,0:T(8,128)(2,1)S(1)}, /*index=5*/s32[]{:T(128)}) while((s32[]{:T(128)}, bf16[8,8,32,384]{3,2,1,0:T(8,128)(2,1)}, bf16[8,8,32,4,128]{4,3,2,1,0:T(4,128)(2,1)}, ...), condition=%wide.region_6.7_spmd, body=%wide.region_5.6_spmd.sunk | while | flops 102237472 | bytes 10622801 | solution.py:15
  430.5 3.3 fusion.47
  437.7 3.3 fusion.47
  444.9 3.3 fusion.47
  452.1 3.3 fusion.47
  466.5 3.3 fusion.47
  473.7 3.2 fusion.47
  480.9 3.3 fusion.47
  484.2 42.5 %all_to_all.32 = bf16[32,64,384]{2,1,0:T(8,128)(2,1)S(1)} all-to-all(bf16[32,64,384]{2,1,0:T(8,128)(2,1)} %bitcast.117), channel_id=1, replica_groups=mesh['dp'=32,'tensor'=16] {'dp'}, dimensions={0} | all-to-all | bytes 3145728 | tf_op jit(solution)/shard_map/all_to_all | solution.py:91
  528.0 59.0 %reduce-scatter.5.cloned.1.call-done = bf16[64,768]{1,0:T(8,128)(2,1)} async-done(((bf16[64,12288]{1,0:T(8,128)(2,1)}), bf16[64,768]{1,0:T(8,128)(2,1)}) %reduce-scatter.5.cloned.1.call-update) | async-done | bytes 98320 | tf_op jit(solution)/shard_map/reduce_scatter | solution.py:92
  (172 shorter events, 75.5 us)
Async XLA Ops:
  6.5 110.9 %copy-start = (bf16[1536]{0:T(1024)(128)(2,1)S(1)}, bf16[1536]{0:T(1024)(128)(2,1)}, u32[]{:S(2)}) copy-start(bf16[1536]{0:T(1024)(128)(2,1)} %param.17) | copy-start | bytes 9220
  6.5 1.9 copy-start.2
  6.5 2.5 copy-start.4
  6.5 2.5 copy-start.5
  11.2 10.4 %copy-start.6 = (s32[64,1,4]{0,2,1:T(4,128)S(1)}, s32[64,1,4]{0,2,1:T(4,128)}, u32[]{:S(2)}) copy-start(s32[64,1,4]{0,2,1:T(4,128)} %param.20) | copy-start | bytes 3076
  11.2 10.5 %copy-start.3 = (bf16[384,1536]{1,0:T(8,128)(2,1)S(1)}, bf16[384,1536]{1,0:T(8,128)(2,1)}, u32[]{:S(2)}) copy-start(bf16[384,1536]{1,0:T(8,128)(2,1)} %param.16) | copy-start | bytes 3538948
  11.2 49.7 %all-to-all-start = ((bf16[64,32,384]{2,0,1:T(8,128)(2,1)}), bf16[64,32,384]{2,0,1:T(8,128)(2,1)}, u32[]{:S(2)}, u32[]{:S(2)}) async-start(bf16[64,32,384]{2,0,1:T(8,128)(2,1)} %bitcast.85), calls=%async_computation | async-start | bytes 3145728 | tf_op jit(solution)/shard_map/all_to_all | solution.py:69
  21.6 315.8 %reduce-scatter.3.cloned.1.call-start = ((), (), s32[]{:S(2)}) async-start(), calls=%async_computation.4 | async-start | bytes 2162688 | tf_op jit(solution)/shard_map/reduce_scatter | solution.py:77
  116.6 0.7 copy-start.8
  116.6 306.0 %all-gather.2.cloned.1.call-start = ((), (), s32[]{:S(2)}) async-start(), calls=%async_computation.5 | async-start | bytes 2162688 | tf_op jit(solution)/shard_map/all_gather | solution.py:88
  339.0 248.0 %reduce-scatter.5.cloned.1.call-start = ((), (), s32[]{:S(2)}) async-start(), calls=%async_computation.6 | async-start | bytes 1671168 | tf_op jit(solution)/shard_map/reduce_scatter | solution.py:92
  339.1 87.5 %copy-start.1 = (bf16[1536,384]{1,0:T(8,128)(2,1)S(1)}, bf16[1536,384]{1,0:T(8,128)(2,1)}, u32[]{:S(2)}) copy-start(bf16[1536,384]{1,0:T(8,128)(2,1)} %param.18) | copy-start | bytes 3538948
  526.7 1.4 copy-start.7
Sparse Core Ops, SparseCore 0:
  116.7 220.6 reduce-scatter.2
  341.0 81.5 all-gather.1
  528.1 58.8 reduce-scatter.4
where the time goes:
time: 596 us; the launch traced here: 595 us
  waiting for transfers between devices  398 us (67%)
  local copies, waits for them, and re-layouts  69.3 us (12%)
  matrix products  54.5 us (9%)
  blocking collectives  42.5 us (7%)
  between operations  13.3 us (2%)
  starting transfers between devices  10.5 us (2%)
  other arithmetic  6.56 us (1%)
    reduce_scatter x1, waiting for transfers between devices, body(): lax.psum_scatter(select_up(columns, ids, up_table).astype(jnp.bfloat16),...  220 us
    all_gather x1, waiting for transfers between devices, body(): act = lax.all_gather(act_own, 'dp', axis=0, tiled=True)  83.5 us
    reduce_scatter x1, waiting for transfers between devices, body(): lax.psum_scatter(returned.astype(jnp.float32).astype(jnp.bfloat16), 'tens...  59 us
    all_to_all x1, blocking collectives, body(): lax.all_to_all(branch, 'dp', split_axis=0, concat_axis=1, tiled=True)  42.5 us
    all_to_all x1, waiting for transfers between devices, body(): lax.all_to_all(normed, 'dp', split_axis=1, concat_axis=0, tiled=True)  36.1 us
    dot_general x8, matrix products, step(): jnp.einsum('grd,dgcb->grcb', block_rows, chosen, preferred_element_type=j...  28.3 us
    dot_general x8, matrix products, step(): jnp.einsum('grcb,gcbd->grd', block_act, chosen, preferred_element_type=jn...  26 us
    gather x8, local copies, waits for them, and re-layouts, step(): chosen = jnp.take(down_table, block_ids, axis=0)  20.9 us
  transfers between devices with their start and end apart: 4, of which 4 were waited for; matrix products, arithmetic and copies ran while one was open for 1% of the time, Pallas kernels for 0%

commit v1 on v0

--- a/solution.py
+++ b/solution.py
@@ -6,6 +6,11 @@
 
 BLOCK = 128
 GROUP = 32
+
+
+def gather_by_exchange(value, axis, dim):
+    copies = jnp.concatenate([value] * lax.axis_size(axis), axis=dim)
+    return lax.all_to_all(copies, axis, dim, dim, tiled=True)
 
 
 def in_blocks(step_fn, arrays):
@@ -85,7 +90,7 @@
     own_ids = lax.dynamic_slice_in_dim(ids, first, per_dev, 0)
     own_valid = lax.dynamic_slice_in_dim(valid, first, per_dev, 0)
     act_own = activate(pre_own, own_ids, own_valid, bias_table)
-    act = lax.all_gather(act_own, "dp", axis=0, tiled=True)
+    act = gather_by_exchange(act_own, "dp", 0)
     branch = select_down(act, ids, down_table)
     branch = branch.astype(jnp.bfloat16)
     returned = lax.all_to_all(branch, "dp", split_axis=0, concat_axis=1, tiled=True)

time: 596 us -> 566 us (0.950)
  waiting for transfers between devices: 398 us -> 359 us
  starting transfers between devices: 10.5 us -> 18.7 us
    all_gather x1 -> x0, waiting for transfers between devices: 83.5 us -> none  [body(): act = lax.all_gather(act_own, 'dp', axis=0, tiled=True)]
    all_to_all x0 -> x1, waiting for transfers between devices: none -> 44.6 us  [gather_by_exchange(): return lax.all_to_all(copies, axis, dim, dim, tiled=True)]
    all_to_all x0 -> x1, starting transfers between devices: none -> 8.25 us  [gather_by_exchange(): return lax.all_to_all(copies, axis, dim, dim, tiled=True)]
where the time goes in v1:
time: 566 us; the launch traced here: 565 us
  waiting for transfers between devices  359 us (63%)
  local copies, waits for them, and re-layouts  70.8 us (13%)
  matrix products  54.5 us (10%)
  blocking collectives  41.9 us (7%)
  starting transfers between devices  18.7 us (3%)
  between operations  13.8 us (2%)
  other arithmetic  5.93 us (1%)
    reduce_scatter x1, waiting for transfers between devices, body(): lax.psum_scatter(select_up(columns, ids, up_table).astype(jnp.bfloat16),...  220 us
    reduce_scatter x1, waiting for transfers between devices, body(): lax.psum_scatter(returned.astype(jnp.float32).astype(jnp.bfloat16), 'tens...  58.9 us
    all_to_all x1, waiting for transfers between devices, gather_by_exchange(): return lax.all_to_all(copies, axis, dim, dim, tiled=True)  44.6 us
    all_to_all x1, blocking collectives, body(): lax.all_to_all(branch, 'dp', split_axis=0, concat_axis=1, tiled=True)  41.9 us
    all_to_all x1, waiting for transfers between devices, body(): lax.all_to_all(normed, 'dp', split_axis=1, concat_axis=0, tiled=True)  36.1 us
    dot_general x8, matrix products, step(): jnp.einsum('grd,dgcb->grcb', block_rows, chosen, preferred_element_type=j...  28.3 us
    dot_general x8, matrix products, step(): jnp.einsum('grcb,gcbd->grd', block_act, chosen, preferred_element_type=jn...  26 us
    gather x8, local copies, waits for them, and re-layouts, step(): chosen = jnp.take(down_table, block_ids, axis=0)  20.9 us
  transfers between devices with their start and end apart: 4, of which 4 were waited for; matrix products, arithmetic and copies ran while one was open for 1% of the time, Pallas kernels for 0%

profile of v1, /device:TPU:6, one launch (start us, length us, event | category | flops | bytes accessed | tf_op | source)
XLA Modules:
  0.0 565.2 jit_solution(15619108084589416661)
XLA Ops:
  11.2 10.4 %all-to-all-start = ((bf16[64,32,384]{2,0,1:T(8,128)(2,1)}), bf16[64,32,384]{2,0,1:T(8,128)(2,1)}, u32[]{:S(2)}, u32[]{:S(2)}) async-start(bf16[64,32,384]{2,0,1:T(8,128)(2,1)} %bitcast.88), calls=%async_computation | async-start | bytes 3145728 | tf_op jit(solution)/shard_map/all_to_all | solution.py:74
  24.8 36.1 %all-to-all-done = bf16[64,32,384]{2,0,1:T(8,128)(2,1)} async-done(((bf16[64,32,384]{2,0,1:T(8,128)(2,1)}), bf16[64,32,384]{2,0,1:T(8,128)(2,1)}, u32[]{:S(2)}, u32[]{:S(2)}) %all-to-all-start) | async-done | bytes 1572896 | tf_op jit(solution)/shard_map/all_to_all | solution.py:74
  60.9 51.3 %while.20 = (s32[]{:T(128)}, bf16[8,8,32,4,128]{4,2,3,1,0:T(8,128)(2,1)}, bf16[8,8,32,384]{3,2,1,0:T(8,128)(2,1)}, s32[8,8,4]{1,2,0:T(4,128)S(1)}, bf16[384,12,128]{2,0,1:T(8,128)(2,1)S(1)}, /*index=5*/s32[]{:T(128)}) while((s32[]{:T(128)}, bf16[8,8,32,4,128]{4,2,3,1,0:T(8,128)(2,1)}, bf16[8,8,32,384]{3,2,1,0:T(8,128)(2,1)}, ...), condition=%wide.region_3.4_spmd, body=%wide.region_2.3_spmd.sunk | while | flops 102237472 | bytes 10164557 | solution.py:20
  63.8 3.5 fusion.46
  70.2 3.6 fusion.46
  76.6 3.5 fusion.46
  83.0 3.5 fusion.46
  89.4 3.5 fusion.46
  95.8 3.5 fusion.46
  102.2 3.5 fusion.46
  108.7 3.5 fusion.46
  117.6 219.8 %reduce-scatter.3.cloned.1.call-done = bf16[64,512]{1,0:T(8,128)(2,1)} async-done(((bf16[2048,512]{1,0:T(8,128)(2,1)}), bf16[64,512]{1,0:T(8,128)(2,1)}) %reduce-scatter.3.cloned.1.call-update) | async-done | bytes 65552 | tf_op jit(solution)/shard_map/reduce_scatter | solution.py:82
  340.1 8.2 %all-to-all-start.1 = ((bf16[32,64,512]{2,1,0:T(8,128)(2,1)}), bf16[32,64,512]{2,1,0:T(8,128)(2,1)}, u32[]{:S(2)}, u32[]{:S(2)}) async-start(bf16[32,64,512]{2,1,0:T(8,128)(2,1)} %bitcast.120), calls=%async_computation.2 | async-start | bytes 4194304 | tf_op jit(solution)/shard_map/all_to_all | solution.py:13
  348.5 44.6 %all-to-all-done.1 = bf16[32,64,512]{2,1,0:T(8,128)(2,1)} async-done(((bf16[32,64,512]{2,1,0:T(8,128)(2,1)}), bf16[32,64,512]{2,1,0:T(8,128)(2,1)}, u32[]{:S(2)}, u32[]{:S(2)}) %all-to-all-start.1) | async-done | bytes 2097184 | tf_op jit(solution)/shard_map/all_to_all | solution.py:13
  393.1 4.0 reshape_reshape.9
  397.1 57.5 %while.21 = (s32[]{:T(128)}, bf16[8,8,32,384]{3,2,1,0:T(8,128)(2,1)}, bf16[8,8,32,4,128]{4,3,2,1,0:T(4,128)(2,1)}, s32[8,8,4]{1,2,0:T(4,128)S(1)}, bf16[12,128,384]{2,1,0:T(8,128)(2,1)S(1)}, /*index=5*/s32[]{:T(128)}) while((s32[]{:T(128)}, bf16[8,8,32,384]{3,2,1,0:T(8,128)(2,1)}, bf16[8,8,32,4,128]{4,3,2,1,0:T(4,128)(2,1)}, ...), condition=%wide.region_6.7_spmd, body=%wide.region_5.6_spmd.sunk | while | flops 102237472 | bytes 10622801 | solution.py:20
  401.0 3.3 fusion.48
  408.2 3.3 fusion.48
  415.4 3.3 fusion.48
  422.6 3.3 fusion.48
  444.2 3.2 fusion.48
  451.4 3.2 fusion.48
  454.6 41.9 %all_to_all.41 = bf16[32,64,384]{2,1,0:T(8,128)(2,1)S(1)} all-to-all(bf16[32,64,384]{2,1,0:T(8,128)(2,1)} %bitcast.121), channel_id=1, replica_groups=mesh['dp'=32,'tensor'=16] {'dp'}, dimensions={0} | all-to-all | bytes 3145728 | tf_op jit(solution)/shard_map/all_to_all | solution.py:96
  497.9 58.9 %reduce-scatter.5.cloned.1.call-done = bf16[64,768]{1,0:T(8,128)(2,1)} async-done(((bf16[64,12288]{1,0:T(8,128)(2,1)}), bf16[64,768]{1,0:T(8,128)(2,1)}) %reduce-scatter.5.cloned.1.call-update) | async-done | bytes 98320 | tf_op jit(solution)/shard_map/reduce_scatter | solution.py:97
  (204 shorter events, 79.5 us)
Async XLA Ops:
  6.5 110.8 %copy-start = (bf16[1536]{0:T(1024)(128)(2,1)S(1)}, bf16[1536]{0:T(1024)(128)(2,1)}, u32[]{:S(2)}) copy-start(bf16[1536]{0:T(1024)(128)(2,1)} %param.17) | copy-start | bytes 9220
  6.5 1.9 copy-start.2
  6.5 2.5 copy-start.5
  6.5 2.5 copy-start.6
  11.2 10.4 %copy-start.7 = (s32[64,1,4]{0,2,1:T(4,128)S(1)}, s32[64,1,4]{0,2,1:T(4,128)}, u32[]{:S(2)}) copy-start(s32[64,1,4]{0,2,1:T(4,128)} %param.20) | copy-start | bytes 3076
  11.2 10.5 %copy-start.4 = (bf16[384,1536]{1,0:T(8,128)(2,1)S(1)}, bf16[384,1536]{1,0:T(8,128)(2,1)}, u32[]{:S(2)}) copy-start(bf16[384,1536]{1,0:T(8,128)(2,1)} %param.16) | copy-start | bytes 3538948
  11.2 49.7 %all-to-all-start = ((bf16[64,32,384]{2,0,1:T(8,128)(2,1)}), bf16[64,32,384]{2,0,1:T(8,128)(2,1)}, u32[]{:S(2)}, u32[]{:S(2)}) async-start(bf16[64,32,384]{2,0,1:T(8,128)(2,1)} %bitcast.88), calls=%async_computation | async-start | bytes 3145728 | tf_op jit(solution)/shard_map/all_to_all | solution.py:74
  21.6 315.8 %reduce-scatter.3.cloned.1.call-start = ((), (), s32[]{:S(2)}) async-start(), calls=%async_computation.5 | async-start | bytes 2162688 | tf_op jit(solution)/shard_map/reduce_scatter | solution.py:82
  116.6 0.7 copy-start.9
  338.8 1.3 copy-start.3
  340.1 52.9 %all-to-all-start.1 = ((bf16[32,64,512]{2,1,0:T(8,128)(2,1)}), bf16[32,64,512]{2,1,0:T(8,128)(2,1)}, u32[]{:S(2)}, u32[]{:S(2)}) async-start(bf16[32,64,512]{2,1,0:T(8,128)(2,1)} %bitcast.120), calls=%async_computation.2 | async-start | bytes 4194304 | tf_op jit(solution)/shard_map/all_to_all | solution.py:13
  348.4 208.4 %reduce-scatter.5.cloned.1.call-start = ((), (), s32[]{:S(2)}) async-start(), calls=%async_computation.6 | async-start | bytes 1671168 | tf_op jit(solution)/shard_map/reduce_scatter | solution.py:97
  348.5 48.6 %copy-start.1 = (bf16[1536,384]{1,0:T(8,128)(2,1)S(1)}, bf16[1536,384]{1,0:T(8,128)(2,1)}, u32[]{:S(2)}) copy-start(bf16[1536,384]{1,0:T(8,128)(2,1)} %param.18) | copy-start | bytes 3538948
  496.5 1.4 copy-start.8
Sparse Core Ops, SparseCore 0:
  116.7 220.6 reduce-scatter.2
  498.0 58.7 reduce-scatter.4
